TPU v7x, 32 devices: a whole 2x2x4 slice. The times are simulated.
32 devices in a mesh: atom: 8 (over z, y), energy: 4 (over x, core).
Axes of the slice: x: 2, y: 2, z: 4, core: 2. Of those that a mesh axis runs over, the one named last changes fastest.
Arguments:
- green: bfloat16 [16, 2, 12, 12, 512], P('atom', None, None, None, 'energy'), may hold values from -6 to 6
- coupling: bfloat16 [16, 34, 2, 12, 12], P('atom'), may hold values from -0.5 to 0.5
- neighbours: int32 [16, 34], P('atom'), may hold values from 0 to 15, as said below
- offsets: int32 [70], replicated, may hold values from 1 to 48, as said below
- w_emit: float32 [70], replicated, may hold values from 0.02 to 0.2
- w_absorb: float32 [70], replicated, may hold values from 0.02 to 0.2
Outputs:
- self_energy: float32 [16, 2, 12, 12, 512], P('atom', None, None, None, 'energy')
Inputs may be any that keep to these rules, and one draw needn't show every extreme that they name: neighbours[a, k] lies among the atoms a // 2 - 1, a // 2, a // 2 + 1 times 2 plus 0 to 1, that is, among the atoms of the same index of atom or of an index one away. `offsets`: some frequency equals 48.
All inputs are finite; a program needn't handle non-finite values.
Results may differ from a plain program's by a relative error of at most 0.0028.
Values may be sent and summed in bfloat16 or wider, within the bound.
A program may use at most 64 MiB of HBM per device.

v0:
```python
import jax
import jax.numpy as jnp
from jax import lax
from jax.sharding import PartitionSpec as P


def extended(cells, sides, width):
    for axis, dim in sides:
        count = lax.axis_size(axis)
        ends = count - 1
        head = lax.slice_in_dim(cells, 0, width, axis=dim)
        tail = lax.slice_in_dim(cells, cells.shape[dim] - width, cells.shape[dim], axis=dim)
        cells = jnp.concatenate(
            [
                lax.ppermute(tail, axis, [(i, (i + 1) % count) for i in range(ends)]),
                cells,
                lax.ppermute(head, axis, [((i + 1) % count, i) for i in range(ends)]),
            ],
            axis=dim,
        )
    return cells


def passed_along(value, axis, steps):
    count = lax.axis_size(axis)
    initial, last = (max(0, -steps), min(count, count - steps))
    return lax.ppermute(value, axis, [(source, source + steps) for source in range(initial, last)])


def couple(blocks, gathered):
    f32 = jnp.float32
    x_re = jnp.einsum(
        "kij,kjle->kile", blocks[:, 0], gathered[:, 0], preferred_element_type=f32
    ) - jnp.einsum("kij,kjle->kile", blocks[:, 1], gathered[:, 1], preferred_element_type=f32)
    x_im = jnp.einsum(
        "kij,kjle->kile", blocks[:, 0], gathered[:, 1], preferred_element_type=f32
    ) + jnp.einsum("kij,kjle->kile", blocks[:, 1], gathered[:, 0], preferred_element_type=f32)
    x_re = x_re.astype(jnp.bfloat16)
    x_im = x_im.astype(jnp.bfloat16)
    p_re = jnp.einsum("kile,kml->ime", x_re, blocks[:, 0], preferred_element_type=f32) + jnp.einsum(
        "kile,kml->ime", x_im, blocks[:, 1], preferred_element_type=f32
    )
    p_im = jnp.einsum("kile,kml->ime", x_im, blocks[:, 0], preferred_element_type=f32) - jnp.einsum(
        "kile,kml->ime", x_re, blocks[:, 1], preferred_element_type=f32
    )
    return jnp.stack([p_re, p_im])


def make_kernel(spread_diff, offsets, w_emit, w_absorb):
    kernel = jnp.sum(
        jnp.where(spread_diff[:, :, None] == offsets, w_emit, jnp.float32(0.0)), axis=2
    )
    return kernel + jnp.sum(
        jnp.where(spread_diff[:, :, None] == -offsets, w_absorb, jnp.float32(0.0)), axis=2
    )


def shards(green, coupling, neighbours, offsets, w_emit, w_absorb):
    hi = lax.Precision.HIGHEST
    atoms_here = green.shape[0]
    points = green.shape[-1]
    reach = points * 3 // 8
    window = extended(green, (("atom", 0),), atoms_here)
    local_ids = neighbours - (lax.axis_index("atom") - 1) * atoms_here

    def one_atom(packed):
        blocks, listed = packed
        gathered = jnp.take(window, listed, axis=0)
        return couple(blocks, gathered)

    coupled = lax.map(one_atom, (coupling, local_ids))
    extent = points + 2 * reach
    back_diff = jnp.arange(points, dtype=jnp.int32)[:, None] - (
        jnp.arange(extent, dtype=jnp.int32)[None, :] - reach
    )
    kernel = make_kernel(back_diff, offsets, w_emit, w_absorb)
    spread_rows = jnp.dot(
        coupled.reshape(-1, points), kernel, precision=hi, preferred_element_type=jnp.float32
    )
    result = spread_rows[:, reach : reach + points]
    from_lower = passed_along(spread_rows[:, reach + points :], "energy", 1)
    from_upper = passed_along(spread_rows[:, :reach].astype(jnp.bfloat16), "energy", -1).astype(
        jnp.float32
    )
    result = result.at[:, :reach].add(from_lower)
    result = result.at[:, points - reach :].add(from_upper)
    return result.reshape(coupled.shape)


def solution(mesh):
    return jax.shard_map(
        shards,
        mesh=mesh,
        in_specs=(
            P("atom", None, None, None, "energy"),
            P("atom", None, None, None, None),
            P("atom", None),
            P(),
            P(),
            P(),
        ),
        out_specs=P("atom", None, None, None, "energy"),
        check_vma=False,
    )
```

profile of v0, /device:TPU:9, one launch (start us, length us, event | category | flops | bytes accessed | tf_op | source)
XLA Modules:
  0.0 78.6 jit_solution(17594882063020760023)
XLA Ops:
  0.0 3.1 %collective-permute-start = (bf16[2,2,12,12,128]{4,1,3,2,0:T(2,128)(2,1)}, bf16[2,2,12,12,128]{4,1,3,2,0:T(2,128)(2,1)S(1)}, u32[]{:S(2)}, u32[]{:S(2)}) collective-permute-start(bf16[2,2,12,12,128]{4,1,3,2,0:T(2,128)(2,1)} %param.12), channel_id=1, source_target_pairs={{0,4},{4,8},{8,12},{12,16},{16,20},{20,24},{24,28},{1,5},{5,9},{9,... | collective-permute-start | bytes 442376 | tf_op jit(solution)/shard_map/ppermute | solution.py:15
  3.1 3.0 %collective-permute-start.1 = (bf16[2,2,12,12,128]{4,1,3,2,0:T(2,128)(2,1)}, bf16[2,2,12,12,128]{4,1,3,2,0:T(2,128)(2,1)S(1)}, u32[]{:S(2)}, u32[]{:S(2)}) collective-permute-start(bf16[2,2,12,12,128]{4,1,3,2,0:T(2,128)(2,1)} %param.12), channel_id=1, source_target_pairs={{4,0},{8,4},{12,8},{16,12},{20,16},{24,20},{28,24},{5,1},{9,5},{13... | collective-permute-start | bytes 442376 | tf_op jit(solution)/shard_map/ppermute | solution.py:17
  7.0 3.2 %select_reduce_fusion = (f32[128,224]{0,1:T(8,128)S(1)}, f32[128,224]{0,1:T(8,128)}) fusion(f32[70]{0:T(128)} %param.17, s32[128,224]{0,1:T(8,128)S(1)} %iota_subtract_fusion, s32[70]{0:T(128)S(1)} %neg.3, f32[70]{0:T(128)} %param.16, s32[70]{0:T(128)} %param.15), kind=kLoop, calls=%fused_computation.47 | loop fusion | flops 11984896 | bytes 345184 | tf_op jit(solution)/shard_map/reduce_sum | solution.py:53
  11.5 1.5 %pad_maximum_fusion = bf16[6,2,12,12,128]{4,1,3,2,0:T(2,128)(2,1)S(1)} fusion(bf16[2,2,12,12,128]{4,1,3,2,0:T(2,128)(2,1)S(1)} %collective-permute-done.1, bf16[2,2,12,12,128]{4,1,3,2,0:T(2,128)(2,1)} %param.12, bf16[2,2,12,12,128]{4,1,3,2,0:T(2,128)(2,1)S(1)} %collective-permute-done), kind=kLoop, calls=%fused_computation.49 | loop fusion | flops 442368 | bytes 884736 | tf_op jit(solution)/shard_map/concatenate | solution.py:13
  13.0 51.7 %while.12 = (s32[]{:T(128)}, f32[2,2,12,12,128]{4,3,2,1,0:T(8,128)}, bf16[2,34,2,12,12]{1,2,4,3,0:T(2,128)(2,1)}, s32[2,34]{1,0:T(2,128)S(1)}, bf16[6,2,12,12,128]{4,1,3,2,0:T(2,128)(2,1)S(1)}, /*index=5*/s32[]{:T(128)}) while((s32[]{:T(128)}, f32[2,2,12,12,128]{4,3,2,1,0:T(8,128)}, bf16[2,34,2,12,12]{1,2,4,3,0:T(2,128)(2,1)}, ...), condition=%wide.region_1.2_spmd, body=%wide.region_0.1_spmd.sunk | while | flops 124159280 | bytes 48670468 | solution.py:71
  13.0 8.9 %gather_fusion = bf16[34,2,12,12,128]{4,1,3,2,0:T(2,128)(2,1)} fusion(bf16[6,2,12,12,128]{4,1,3,2,0:T(2,128)(2,1)S(1)} %get-tuple-element.137, s32[1024]{0:T(1024)S(1)} %pad_clamp_fusion.2), kind=kCustom, calls=%fused_computation.clone.1 | custom fusion | bytes 5013640 | tf_op jit(solution)/shard_map/while/body/eval_jaxpr/jit(_take)/gather | solution.py:68
  21.9 2.4 %copy_select_fusion.2 = bf16[34,2,12,12,128]{4,2,3,0,1:T(8,128)(2,1)S(1)} fusion(bf16[34,2,12,12,128]{4,1,3,2,0:T(2,128)(2,1)} %gather_fusion, pred[34]{0:T(512)(128)(4,1)S(1)} %compare_and_fusion.2), kind=kLoop, calls=%fused_computation.1.clone.1 | loop fusion | flops 1253376 | bytes 5013538 | tf_op jit(solution)/shard_map/while/body/eval_jaxpr/jit(_take)/select_n | solution.py:68
  24.4 1.1 %copy.89 = bf16[1,34,2,12,12]{4,3,1,2,0:T(8,128)(2,1)} copy(bf16[1,34,2,12,12]{1,2,4,3,0:T(2,128)(2,1)S(1)} %constant_dynamic-slice_fusion.3) | data formatting | bytes 39168 | tf_op jit(solution)/shard_map/while/body/jit(dynamic_index_in_dim)/dynamic_slice | solution.py:71
  25.4 1.5 %fusion.88 = f32[34,12,12,128]{3,1,2,0:T(8,128)S(1)} fusion(bf16[34,2,12,12,128]{4,2,3,0,1:T(8,128)(2,1)S(1)} %copy_select_fusion.2, bf16[34,2,12,12]{3,2,0,1:T(8,128)(2,1)} %bitcast.126), kind=kOutput, calls=%fused_computation.7.clone.1 | convolution fusion | flops 15040512 | bytes 4317184 | tf_op jit(solution)/shard_map/while/body/eval_jaxpr/kij,kjle->kile/dot_general | solution.py:35
  27.0 1.7 %add_convert_fusion.2 = bf16[34,12,12,128]{3,1,2,0:T(8,128)(2,1)} fusion(f32[34,12,12,128]{3,1,2,0:T(8,128)S(1)} %fusion.88, bf16[34,2,12,12,128]{4,2,3,0,1:T(8,128)(2,1)S(1)} %copy_select_fusion.2, bf16[34,2,12,12]{3,2,0,1:T(8,128)(2,1)S(1)} %bitcast.127), kind=kOutput, calls=%fused_computation.2.clone.1 | convolution fusion | flops 16293888 | bytes 6406144 | tf_op jit(solution)/shard_map/while/body/eval_jaxpr/kij,kjle->kile/dot_general | solution.py:37
  29.3 1.8 %subtract_convert_fusion.2 = bf16[34,12,12,128]{3,1,2,0:T(8,128)(2,1)} fusion(f32[34,12,12,128]{3,1,2,0:T(8,128)S(1)} %fusion.86, bf16[34,2,12,12,128]{4,2,3,0,1:T(8,128)(2,1)S(1)} %copy_select_fusion.2, bf16[34,2,12,12]{3,2,0,1:T(8,128)(2,1)S(1)} %bitcast.129), kind=kOutput, calls=%fused_computation.3.clone.1 | convolution fusion | flops 16293888 | bytes 6406144 | tf_op jit(solution)/shard_map/while/body/eval_jaxpr/kij,kjle->kile/dot_general | solution.py:34
  31.4 2.4 %fusion.90 = f32[12,12,128]{2,0,1:T(8,128)S(1)} fusion(bf16[34,12,12,128]{3,1,2,0:T(8,128)(2,1)} %subtract_convert_fusion.2, bf16[34,12,12]{0,1,2:T(8,128)(2,1)S(1)} %copy.91), kind=kOutput, calls=%fused_computation.16.clone.1 | convolution fusion | flops 15040512 | bytes 1336896 | tf_op jit(solution)/shard_map/while/body/eval_jaxpr/kile,kml->ime/dot_general | solution.py:40
  34.9 2.3 %fusion.87 = f32[12,12,128]{2,0,1:T(8,128)S(1)} fusion(bf16[34,12,12,128]{3,1,2,0:T(8,128)(2,1)} %subtract_convert_fusion.2, bf16[34,12,12]{0,1,2:T(8,128)(2,1)S(1)} %copy.90), kind=kOutput, calls=%fused_computation.17.clone.1 | convolution fusion | flops 15040512 | bytes 1336896 | tf_op jit(solution)/shard_map/while/body/eval_jaxpr/kile,kml->ime/dot_general | solution.py:43
  38.9 8.9 %gather_fusion = bf16[34,2,12,12,128]{4,1,3,2,0:T(2,128)(2,1)} fusion(bf16[6,2,12,12,128]{4,1,3,2,0:T(2,128)(2,1)S(1)} %get-tuple-element.137, s32[1024]{0:T(1024)S(1)} %pad_clamp_fusion.2), kind=kCustom, calls=%fused_computation.clone.1 | custom fusion | bytes 5013640 | tf_op jit(solution)/shard_map/while/body/eval_jaxpr/jit(_take)/gather | solution.py:68
  47.8 2.4 %copy_select_fusion.2 = bf16[34,2,12,12,128]{4,2,3,0,1:T(8,128)(2,1)S(1)} fusion(bf16[34,2,12,12,128]{4,1,3,2,0:T(2,128)(2,1)} %gather_fusion, pred[34]{0:T(512)(128)(4,1)S(1)} %compare_and_fusion.2), kind=kLoop, calls=%fused_computation.1.clone.1 | loop fusion | flops 1253376 | bytes 5013538 | tf_op jit(solution)/shard_map/while/body/eval_jaxpr/jit(_take)/select_n | solution.py:68
  51.3 1.5 %fusion.88 = f32[34,12,12,128]{3,1,2,0:T(8,128)S(1)} fusion(bf16[34,2,12,12,128]{4,2,3,0,1:T(8,128)(2,1)S(1)} %copy_select_fusion.2, bf16[34,2,12,12]{3,2,0,1:T(8,128)(2,1)} %bitcast.126), kind=kOutput, calls=%fused_computation.7.clone.1 | convolution fusion | flops 15040512 | bytes 4317184 | tf_op jit(solution)/shard_map/while/body/eval_jaxpr/kij,kjle->kile/dot_general | solution.py:35
  52.9 1.7 %add_convert_fusion.2 = bf16[34,12,12,128]{3,1,2,0:T(8,128)(2,1)} fusion(f32[34,12,12,128]{3,1,2,0:T(8,128)S(1)} %fusion.88, bf16[34,2,12,12,128]{4,2,3,0,1:T(8,128)(2,1)S(1)} %copy_select_fusion.2, bf16[34,2,12,12]{3,2,0,1:T(8,128)(2,1)S(1)} %bitcast.127), kind=kOutput, calls=%fused_computation.2.clone.1 | convolution fusion | flops 16293888 | bytes 6406144 | tf_op jit(solution)/shard_map/while/body/eval_jaxpr/kij,kjle->kile/dot_general | solution.py:37
  55.2 1.8 %subtract_convert_fusion.2 = bf16[34,12,12,128]{3,1,2,0:T(8,128)(2,1)} fusion(f32[34,12,12,128]{3,1,2,0:T(8,128)S(1)} %fusion.86, bf16[34,2,12,12,128]{4,2,3,0,1:T(8,128)(2,1)S(1)} %copy_select_fusion.2, bf16[34,2,12,12]{3,2,0,1:T(8,128)(2,1)S(1)} %bitcast.129), kind=kOutput, calls=%fused_computation.3.clone.1 | convolution fusion | flops 16293888 | bytes 6406144 | tf_op jit(solution)/shard_map/while/body/eval_jaxpr/kij,kjle->kile/dot_general | solution.py:34
  57.2 2.4 %fusion.90 = f32[12,12,128]{2,0,1:T(8,128)S(1)} fusion(bf16[34,12,12,128]{3,1,2,0:T(8,128)(2,1)} %subtract_convert_fusion.2, bf16[34,12,12]{0,1,2:T(8,128)(2,1)S(1)} %copy.91), kind=kOutput, calls=%fused_computation.16.clone.1 | convolution fusion | flops 15040512 | bytes 1336896 | tf_op jit(solution)/shard_map/while/body/eval_jaxpr/kile,kml->ime/dot_general | solution.py:40
  60.8 2.3 %fusion.87 = f32[12,12,128]{2,0,1:T(8,128)S(1)} fusion(bf16[34,12,12,128]{3,1,2,0:T(8,128)(2,1)} %subtract_convert_fusion.2, bf16[34,12,12]{0,1,2:T(8,128)(2,1)S(1)} %copy.90), kind=kOutput, calls=%fused_computation.17.clone.1 | convolution fusion | flops 15040512 | bytes 1336896 | tf_op jit(solution)/shard_map/while/body/eval_jaxpr/kile,kml->ime/dot_general | solution.py:43
  65.7 1.5 %fusion.50 = f32[576,224]{0,1:T(8,128)S(1)} fusion(f32[576,128]{1,0:T(8,128)S(1)} %reshape.115, f32[128,224]{0,1:T(8,128)} %get-tuple-element.73, f32[128,224]{0,1:T(8,128)S(1)} %get-tuple-element.72), kind=kOutput, calls=%fused_computation.55 | convolution fusion | flops 198209536 | bytes 1040384 | tf_op jit(solution)/shard_map/dot_general | solution.py:77
  67.3 4.0 %collective-permute-start.2 = (f32[576,48]{0,1:T(8,128)S(1)}, f32[576,48]{0,1:T(8,128)S(1)}, u32[]{:S(2)}, u32[]{:S(2)}) collective-permute-start(f32[576,48]{0,1:T(8,128)S(1)} %slice.82), channel_id=1, source_target_pairs={{0,1},{1,2},{2,3},{4,5},{5,6},{6,7},{8,9},{9,10},{10,11},{12,13},{... | collective-permute-start | bytes 331784 | tf_op jit(solution)/shard_map/ppermute | solution.py:27
  71.9 1.9 %collective-permute-start.3 = (bf16[576,48]{0,1:T(8,128)(2,1)S(1)}, bf16[576,48]{0,1:T(8,128)(2,1)S(1)}, u32[]{:S(2)}, u32[]{:S(2)}) collective-permute-start(bf16[576,48]{0,1:T(8,128)(2,1)S(1)} %slice.114), channel_id=1, source_target_pairs={{1,0},{2,1},{3,2},{5,4},{6,5},{7,6},{9,8},{10,9},{11,10},{13,12},{... | collective-permute-start | bytes 165896 | tf_op jit(solution)/shard_map/ppermute | solution.py:27
  74.5 2.9 %collective-permute-done.3 = bf16[576,48]{0,1:T(8,128)(2,1)S(1)} collective-permute-done((bf16[576,48]{0,1:T(8,128)(2,1)S(1)}, bf16[576,48]{0,1:T(8,128)(2,1)S(1)}, u32[]{:S(2)}, u32[]{:S(2)}) %collective-permute-start.3) | collective-permute-done | bytes 55328 | tf_op jit(solution)/shard_map/ppermute | solution.py:27
  (69 shorter events, 14.0 us)
Async XLA Ops:
  0.0 10.8 %collective-permute-start = (bf16[2,2,12,12,128]{4,1,3,2,0:T(2,128)(2,1)}, bf16[2,2,12,12,128]{4,1,3,2,0:T(2,128)(2,1)S(1)}, u32[]{:S(2)}, u32[]{:S(2)}) collective-permute-start(bf16[2,2,12,12,128]{4,1,3,2,0:T(2,128)(2,1)} %param.12), channel_id=1, source_target_pairs={{0,4},{4,8},{8,12},{12,16},{16,20},{20,24},{24,28},{1,5},{5,9},{9,... | collective-permute-start | bytes 442376 | tf_op jit(solution)/shard_map/ppermute | solution.py:15
  3.1 8.3 %collective-permute-start.1 = (bf16[2,2,12,12,128]{4,1,3,2,0:T(2,128)(2,1)}, bf16[2,2,12,12,128]{4,1,3,2,0:T(2,128)(2,1)S(1)}, u32[]{:S(2)}, u32[]{:S(2)}) collective-permute-start(bf16[2,2,12,12,128]{4,1,3,2,0:T(2,128)(2,1)} %param.12), channel_id=1, source_target_pairs={{4,0},{8,4},{12,8},{16,12},{20,16},{24,20},{28,24},{5,1},{9,5},{13... | collective-permute-start | bytes 442376 | tf_op jit(solution)/shard_map/ppermute | solution.py:17
  13.0 8.9 %copy-start = (bf16[6,2,12,12,128]{4,1,3,2,0:T(2,128)(2,1)}, bf16[6,2,12,12,128]{4,1,3,2,0:T(2,128)(2,1)S(1)}, u32[]{:S(2)}) copy-start(bf16[6,2,12,12,128]{4,1,3,2,0:T(2,128)(2,1)S(1)} %get-tuple-element.137) | copy-start | bytes 1327108 | tf_op jit(solution)/shard_map/while
  21.9 2.4 %copy-start.4 = (bf16[2,34,2,12,12]{1,2,4,3,0:T(2,128)(2,1)S(1)}, bf16[2,34,2,12,12]{1,2,4,3,0:T(2,128)(2,1)}, u32[]{:S(2)}) copy-start(bf16[2,34,2,12,12]{1,2,4,3,0:T(2,128)(2,1)} %get-tuple-element.135) | copy-start | bytes 117508 | tf_op jit(solution)/shard_map/while
  25.4 1.5 %copy-start.3 = (bf16[1,34,2,12,12]{4,3,1,2,0:T(8,128)(2,1)S(1)}, bf16[1,34,2,12,12]{4,3,1,2,0:T(8,128)(2,1)}, u32[]{:S(2)}) copy-start(bf16[1,34,2,12,12]{4,3,1,2,0:T(8,128)(2,1)} %copy.89) | copy-start | bytes 58756 | tf_op jit(solution)/shard_map/while
  31.1 3.0 %copy-start.2 = (bf16[34,12,12,128]{3,1,2,0:T(8,128)(2,1)S(1)}, bf16[34,12,12,128]{3,1,2,0:T(8,128)(2,1)}, u32[]{:S(2)}) copy-start(bf16[34,12,12,128]{3,1,2,0:T(8,128)(2,1)} %add_convert_fusion.2) | copy-start | bytes 3760132 | tf_op jit(solution)/shard_map/while
  34.0 4.0 %copy-start.5 = (f32[2,2,12,12,128]{4,3,2,1,0:T(8,128)S(1)}, f32[2,2,12,12,128]{4,3,2,1,0:T(8,128)}, u32[]{:S(2)}) copy-start(f32[2,2,12,12,128]{4,3,2,1,0:T(8,128)} %get-tuple-element.128) | copy-start | bytes 884740 | tf_op jit(solution)/shard_map/while
  34.1 4.8 %copy-start.1 = (bf16[6,2,12,12,128]{4,1,3,2,0:T(2,128)(2,1)S(1)}, bf16[6,2,12,12,128]{4,1,3,2,0:T(2,128)(2,1)}, u32[]{:S(2)}) copy-start(bf16[6,2,12,12,128]{4,1,3,2,0:T(2,128)(2,1)} %copy-done) | copy-start | bytes 1327108 | tf_op jit(solution)/shard_map/while
  38.1 0.7 copy-start.6
  38.8 8.9 %copy-start = (bf16[6,2,12,12,128]{4,1,3,2,0:T(2,128)(2,1)}, bf16[6,2,12,12,128]{4,1,3,2,0:T(2,128)(2,1)S(1)}, u32[]{:S(2)}) copy-start(bf16[6,2,12,12,128]{4,1,3,2,0:T(2,128)(2,1)S(1)} %get-tuple-element.137) | copy-start | bytes 1327108 | tf_op jit(solution)/shard_map/while
  47.8 2.4 %copy-start.4 = (bf16[2,34,2,12,12]{1,2,4,3,0:T(2,128)(2,1)S(1)}, bf16[2,34,2,12,12]{1,2,4,3,0:T(2,128)(2,1)}, u32[]{:S(2)}) copy-start(bf16[2,34,2,12,12]{1,2,4,3,0:T(2,128)(2,1)} %get-tuple-element.135) | copy-start | bytes 117508 | tf_op jit(solution)/shard_map/while
  51.3 1.5 %copy-start.3 = (bf16[1,34,2,12,12]{4,3,1,2,0:T(8,128)(2,1)S(1)}, bf16[1,34,2,12,12]{4,3,1,2,0:T(8,128)(2,1)}, u32[]{:S(2)}) copy-start(bf16[1,34,2,12,12]{4,3,1,2,0:T(8,128)(2,1)} %copy.89) | copy-start | bytes 58756 | tf_op jit(solution)/shard_map/while
  56.9 3.0 %copy-start.2 = (bf16[34,12,12,128]{3,1,2,0:T(8,128)(2,1)S(1)}, bf16[34,12,12,128]{3,1,2,0:T(8,128)(2,1)}, u32[]{:S(2)}) copy-start(bf16[34,12,12,128]{3,1,2,0:T(8,128)(2,1)} %add_convert_fusion.2) | copy-start | bytes 3760132 | tf_op jit(solution)/shard_map/while
  59.9 4.0 %copy-start.5 = (f32[2,2,12,12,128]{4,3,2,1,0:T(8,128)S(1)}, f32[2,2,12,12,128]{4,3,2,1,0:T(8,128)}, u32[]{:S(2)}) copy-start(f32[2,2,12,12,128]{4,3,2,1,0:T(8,128)} %get-tuple-element.128) | copy-start | bytes 884740 | tf_op jit(solution)/shard_map/while
  59.9 4.8 %copy-start.1 = (bf16[6,2,12,12,128]{4,1,3,2,0:T(2,128)(2,1)S(1)}, bf16[6,2,12,12,128]{4,1,3,2,0:T(2,128)(2,1)}, u32[]{:S(2)}) copy-start(bf16[6,2,12,12,128]{4,1,3,2,0:T(2,128)(2,1)} %copy-done) | copy-start | bytes 1327108 | tf_op jit(solution)/shard_map/while
  63.9 0.7 copy-start.6
  67.3 6.6 %collective-permute-start.2 = (f32[576,48]{0,1:T(8,128)S(1)}, f32[576,48]{0,1:T(8,128)S(1)}, u32[]{:S(2)}, u32[]{:S(2)}) collective-permute-start(f32[576,48]{0,1:T(8,128)S(1)} %slice.82), channel_id=1, source_target_pairs={{0,1},{1,2},{2,3},{4,5},{5,6},{6,7},{8,9},{9,10},{10,11},{12,13},{... | collective-permute-start | bytes 331784 | tf_op jit(solution)/shard_map/ppermute | solution.py:27
  71.9 5.5 %collective-permute-start.3 = (bf16[576,48]{0,1:T(8,128)(2,1)S(1)}, bf16[576,48]{0,1:T(8,128)(2,1)S(1)}, u32[]{:S(2)}, u32[]{:S(2)}) collective-permute-start(bf16[576,48]{0,1:T(8,128)(2,1)S(1)} %slice.114), channel_id=1, source_target_pairs={{1,0},{2,1},{3,2},{5,4},{6,5},{7,6},{9,8},{10,9},{11,10},{13,12},{... | collective-permute-start | bytes 165896 | tf_op jit(solution)/shard_map/ppermute | solution.py:27
where the time goes:
time: 79.2 us; the launch traced here: 78.6 us
  matrix products  25.6 us (32%)
  local copies, waits for them, and re-layouts  24.7 us (31%)
  other arithmetic  12.3 us (16%)
  starting transfers between devices  12.1 us (15%)
  waiting for transfers between devices  3.57 us (5%)
    gather x2, local copies, waits for them, and re-layouts, one_atom(): gathered = jnp.take(window, listed, axis=0)  17.7 us
    ppermute x2, starting transfers between devices, passed_along(): lax.ppermute(value, axis, [(source, source + steps) for source in range(i...  5.88 us
    dot_general x2, matrix products, couple(): jnp.einsum('kile,kml->ime', x_re, blocks[:, 0], preferred_element_type=f32)  4.87 us
    select_n x4, other arithmetic, one_atom(): gathered = jnp.take(window, listed, axis=0)  4.78 us
    dot_general x2, matrix products, couple(): jnp.einsum('kile,kml->ime', x_re, blocks[:, 1], preferred_element_type=f32)  4.58 us
    dot_general x2, matrix products, couple(): jnp.einsum('kij,kjle->kile', blocks[:, 1], gathered[:, 1], preferred_elem...  3.52 us
    dot_general x2, matrix products, couple(): jnp.einsum('kij,kjle->kile', blocks[:, 1], gathered[:, 0], preferred_elem...  3.48 us
    reduce_sum x1, other arithmetic, make_kernel(): jnp.sum(jnp.where(spread_diff[:, :, None] == -offsets, w_absorb, jnp.floa...  3.16 us
  transfers between devices with their start and end apart: 4, of which 2 were waited for; matrix products, arithmetic and copies ran while one was open for 8% of the time, Pallas kernels for 0%

commit v1 on v0

v1 whole, which is shorter than its diff:
```python
import jax
import jax.numpy as jnp
from jax import lax
from jax.experimental import pallas as pl
from jax.experimental.pallas import tpu as pltpu
from jax.sharding import PartitionSpec as P

F32 = jnp.float32
BF16 = jnp.bfloat16
ROWS = 16


def shifted(value, axis, step):
    count = lax.axis_size(axis)
    pairs = [(i, i + step) for i in range(count) if 0 <= i + step < count]
    return lax.ppermute(value, axis, pairs)


def expanders(orb, width):
    half = width // 2
    row = lax.broadcasted_iota(jnp.int32, (2 * ROWS, width), 0)
    col = lax.broadcasted_iota(jnp.int32, (2 * ROWS, width), 1)
    part = (row >= ROWS).astype(jnp.int32)
    entry = row - ROWS * part
    side = (col >= half).astype(jnp.int32)
    outer = (col >> 4) - orb * side
    inner = col & 15
    one, zero = jnp.float32(1), jnp.float32(0)
    at_outer, at_inner = entry == outer, entry == inner
    a1 = jnp.where(at_outer & (part == side), one, zero)
    a2 = jnp.where(at_outer & (part != side), jnp.where(side == 0, one, -one), zero)
    b1 = jnp.where(at_inner & (part == 0), one, zero)
    b2 = jnp.where(at_inner & (part == 1), one, zero)
    return [m.astype(BF16) for m in (a1, a2, b1, b2)]


def build(nb_ref, coup_ref, l_ref, a1_ref, a2_ref, b1_ref, b2_ref, acc_ref):
    atoms, listed = nb_ref.shape
    near, orb, _, width = acc_ref.shape
    first = (lax.axis_index("atom") - 1) * atoms
    mats = expanders(orb, width)
    for a in range(atoms):
        for ref, mat in zip((a1_ref, a2_ref, b1_ref, b2_ref), mats):
            ref[...] = jnp.dot(coup_ref[a], mat, preferred_element_type=F32).reshape(ref.shape)
        acc_ref[...] = jnp.zeros_like(acc_ref)

        def one(k, carry):
            b = nb_ref[a, k] - first
            b1, b2 = b1_ref[k], b2_ref[k]
            for i in range(orb):
                acc_ref[b, i] += a1_ref[k, i : i + 1, :] * b1 + a2_ref[k, i : i + 1, :] * b2
            return carry

        lax.fori_loop(0, listed, one, 0)
        for b in range(near):
            l_ref[a, :, :, b * width : (b + 1) * width] = acc_ref[b].astype(BF16)


def split(x):
    high = x.astype(BF16)
    return high, (x - high.astype(F32)).astype(BF16)


def spread_matrix(off_ref, emit_ref, absorb_ref, points):
    span = 2 * points
    lane = lax.broadcasted_iota(jnp.int32, (8, span), 1)
    line = jnp.zeros((8, span), F32)
    for q in range(off_ref.shape[0]):
        off = off_ref[q]
        line += jnp.where(lane == span - off, emit_ref[q], jnp.float32(0))
        line += jnp.where(lane == off, absorb_ref[q], jnp.float32(0))
    full = jnp.broadcast_to(line[0:1], (points, span))
    return pltpu.roll(full, 0, 1, stride=1, stride_axis=0)


def finish(off_ref, emit_ref, absorb_ref, l_ref, lower_ref, own_ref, upper_ref, out_ref, side_ref, rhs_ref):
    atoms, _, orb, _, points = own_ref.shape
    rhs_ref[...] = jnp.zeros_like(rhs_ref)
    for g, ref in enumerate((lower_ref, own_ref, upper_ref)):
        for a in range(atoms):
            b = g * atoms + a
            re, im = ref[a, 0], ref[a, 1]
            rhs_ref[b, 0, :, 0:orb, :points] = re
            rhs_ref[b, 0, :, 0:orb, points:] = im
            rhs_ref[b, 1, :, 0:orb, :points] = -im
            rhs_ref[b, 1, :, 0:orb, points:] = re
    rows = atoms * orb * ROWS
    depth = l_ref.shape[-1]
    p = jnp.dot(
        l_ref[...].reshape(rows, depth), rhs_ref[...].reshape(depth, 2 * points), preferred_element_type=F32
    )
    t_high, t_low = split(spread_matrix(off_ref, emit_ref, absorb_ref, points))
    for r in range(2):
        high, low = split(p[:, r * points : (r + 1) * points])
        s = jnp.dot(high, t_high, preferred_element_type=F32)
        s += jnp.dot(high, t_low, preferred_element_type=F32)
        s += jnp.dot(low, t_high, preferred_element_type=F32)
        s = s.reshape(atoms, orb, ROWS, 2 * points)
        for a in range(atoms):
            out_ref[a, r] = s[a, :, :orb, :points]
            side_ref[a, r] = s[a, :, :orb, points:].astype(BF16)


def shards(green, coupling, neighbours, offsets, w_emit, w_absorb):
    atoms, _, orb, _, points = green.shape
    listed = neighbours.shape[1]
    reach = points * 3 // 8
    width = 2 * orb * ROWS
    near = 3 * atoms
    vmem, smem = pl.BlockSpec(memory_space=pltpu.VMEM), pl.BlockSpec(memory_space=pltpu.SMEM)
    lower = shifted(green, "atom", 1)
    upper = shifted(green, "atom", -1)
    coup = jnp.pad(
        coupling.transpose(0, 1, 3, 2, 4), ((0, 0), (0, 0), (0, ROWS - orb), (0, 0), (0, ROWS - orb))
    ).reshape(atoms, listed * ROWS, 2 * ROWS)
    expanded = pltpu.VMEM((listed, ROWS, width), F32)
    operator = pl.pallas_call(
        build,
        out_shape=jax.ShapeDtypeStruct((atoms, orb, ROWS, near * width), BF16),
        in_specs=[smem, vmem],
        out_specs=vmem,
        scratch_shapes=[expanded] * 4 + [pltpu.VMEM((near, orb, ROWS, width), F32)],
        compiler_params=pltpu.CompilerParams(vmem_limit_bytes=32 << 20),
        cost_estimate=pl.CostEstimate(flops=30_000_000, bytes_accessed=12_000_000, transcendentals=0),
    )(neighbours, coup)
    result, side = pl.pallas_call(
        finish,
        out_shape=(
            jax.ShapeDtypeStruct(green.shape, F32),
            jax.ShapeDtypeStruct(green.shape, BF16),
        ),
        in_specs=[smem, smem, smem] + [vmem] * 4,
        out_specs=(vmem, vmem),
        scratch_shapes=[pltpu.VMEM((near, 2, orb, ROWS, 2 * points), BF16)],
        compiler_params=pltpu.CompilerParams(vmem_limit_bytes=32 << 20),
    )(offsets, w_emit, w_absorb, operator, lower, green, upper)
    from_lower = shifted(side, "energy", 1)
    from_upper = shifted(side, "energy", -1)
    lane = jnp.arange(points, dtype=jnp.int32)
    result += jnp.where(lane < reach, from_lower, 0).astype(F32)
    return result + jnp.where(lane >= points - reach, from_upper, 0).astype(F32)


def solution(mesh):
    return jax.shard_map(
        shards,
        mesh=mesh,
        in_specs=(
            P("atom", None, None, None, "energy"),
            P("atom", None, None, None, None),
            P("atom", None),
            P(),
            P(),
            P(),
        ),
        out_specs=P("atom", None, None, None, "energy"),
        check_vma=False,
    )
```

time: 79.2 us -> 29.6 us (0.37)
  matrix products: 25.6 us -> 0 us
  local copies, waits for them, and re-layouts: 24.7 us -> 4.13 us
  other arithmetic: 12.3 us -> 0.11 us
  Pallas kernels: 0 us -> 7.54 us
  waiting for transfers between devices: 3.57 us -> 5.1 us
    dot_general x17 -> x0, matrix products: 25.6 us -> none  [the longest x2 4.87 us: couple(): jnp.einsum('kile,kml->ime', x_re, blocks[:, 0], preferred_element_type=f32)]
    gather x2 -> x0, local copies, waits for them, and re-layouts: 17.7 us -> none  [one_atom(): gathered = jnp.take(window, listed, axis=0)]
    pallas_call x0 -> x2, Pallas kernels: none -> 7.54 us  [the longest x1 5.28 us: shards(): pl.pallas_call(build, out_shape=jax.ShapeDtypeStruct((atoms, orb, ROWS, n...]
    select_n x4 -> x0, other arithmetic: 4.78 us -> none  [one_atom(): gathered = jnp.take(window, listed, axis=0)]
    reduce_sum x1 -> x0, other arithmetic: 3.16 us -> none  [make_kernel(): jnp.sum(jnp.where(spread_diff[:, :, None] == -offsets, w_absorb, jnp.floa...]
    unnamed x0 -> x10, local copies, waits for them, and re-layouts: none -> 2.43 us
    dynamic_slice x4 -> x0, local copies, waits for them, and re-layouts: 2.26 us -> none  [shards(): coupled = lax.map(one_atom, (coupling, local_ids))]
    reshape x3 -> x1, local copies, waits for them, and re-layouts: 1.99 us -> 0.26 us  [shards(): coup = jnp.pad(coupling.transpose(0, 1, 3, 2, 4), ((0, 0), (0, 0), (0, RO...]
  transfers between devices with their start and end apart: 4 -> 4, of which waited for: 2 -> 2; matrix products, arithmetic and copies ran while one was open for 8% -> 8% of each run, Pallas kernels for 0% -> 18%
where the time goes in v1:
time: 29.6 us; the launch traced here: 29.3 us
  starting transfers between devices  12.3 us (42%)
  Pallas kernels  7.54 us (25%)
  waiting for transfers between devices  5.1 us (17%)
  local copies, waits for them, and re-layouts  4.13 us (14%)
    ppermute x4, starting transfers between devices, shifted(): return lax.ppermute(value, axis, pairs)  12.3 us
    pallas_call x1, Pallas kernels, shards(): pl.pallas_call(build, out_shape=jax.ShapeDtypeStruct((atoms, orb, ROWS, n...  5.28 us
    ppermute x4, waiting for transfers between devices, shifted(): return lax.ppermute(value, axis, pairs)  5.1 us
    unnamed x10, local copies, waits for them, and re-layouts  2.43 us
    pallas_call x1, Pallas kernels, shards(): pl.pallas_call(finish, out_shape=(jax.ShapeDtypeStruct(green.shape, F32),...  2.25 us
    add x1, local copies, waits for them, and re-layouts, shards(): return result + jnp.where(lane >= points - reach, from_upper, 0).astype(F32)  0.94 us
  transfers between devices with their start and end apart: 4, of which 2 were waited for; matrix products, arithmetic and copies ran while one was open for 8% of the time, Pallas kernels for 18%

profile of v1, /device:TPU:9, one launch (start us, length us, event | category | flops | bytes accessed | tf_op | source)
XLA Modules:
  0.0 29.3 jit_solution(1226135062248736664)
XLA Ops:
  0.0 0.0 copy-start
  0.0 0.9 %copy.14.own_ref = bf16[2,2,12,12,128]{4,3,2,1,0:T(8,128)(2,1)S(1)} copy(bf16[2,2,12,12,128]{4,1,3,2,0:T(2,128)(2,1)} %param.6) | data formatting | bytes 294912 | tf_op args[0]
  1.0 3.1 %collective-permute-start = (bf16[2,2,12,12,128]{4,3,2,1,0:T(8,128)(2,1)S(1)}, bf16[2,2,12,12,128]{4,3,2,1,0:T(8,128)(2,1)S(1)}, u32[]{:S(2)}, u32[]{:S(2)}) collective-permute-start(bf16[2,2,12,12,128]{4,3,2,1,0:T(8,128)(2,1)S(1)} %copy.14.own_ref), channel_id=1, source_target_pairs={{0,4},{4,8},{8,12},{12,16},{16,20},{20,24},{24,28},{1,5},{5,9},{9,... | collective-permute-start | bytes 442376 | tf_op jit(solution)/shard_map/ppermute | solution.py:16
  4.1 3.0 %collective-permute-start.1 = (bf16[2,2,12,12,128]{4,3,2,1,0:T(8,128)(2,1)S(1)}, bf16[2,2,12,12,128]{4,3,2,1,0:T(8,128)(2,1)S(1)}, u32[]{:S(2)}, u32[]{:S(2)}) collective-permute-start(bf16[2,2,12,12,128]{4,3,2,1,0:T(8,128)(2,1)S(1)} %copy.14.own_ref), channel_id=1, source_target_pairs={{4,0},{8,4},{12,8},{16,12},{20,16},{24,20},{28,24},{5,1},{9,5},{13... | collective-permute-start | bytes 442376 | tf_op jit(solution)/shard_map/ppermute | solution.py:16
  7.2 1.5 %copy.20 = bf16[2,34,12,2,12]{4,3,2,1,0:T(2,128)(2,1)S(1)} copy(bf16[2,34,12,2,12]{1,3,4,2,0:T(2,128)(2,1)} %bitcast.1) | data formatting | bytes 78336
  8.6 0.0 copy-start.1
  8.6 0.0 copy-start.2
  8.6 0.0 copy-start.3
  8.7 0.5 %pad.4.clone = bf16[2,34,16,2,16]{4,3,2,1,0:T(2,128)(2,1)S(1)} pad(bf16[2,34,12,2,12]{4,3,2,1,0:T(2,128)(2,1)S(1)} %copy.20, bf16[]{:T(256)} %constant.1.clone.1), padding=0_0x0_0x0_4x0_0x0_4 | pad | bytes 108802 | tf_op jit(solution)/shard_map/jit(_pad)/pad | solution.py:113
  9.2 0.3 reshape.4.coup_ref
  9.4 0.0 copy-done
  9.4 5.3 %shard_map.64.l_ref = bf16[2,12,16,2304]{3,2,1,0:T(8,128)(2,1)S(1)} custom-call(s32[2,34]{1,0:T(2,128)S(1)} %copy-done, bf16[2,544,32]{2,1,0:T(8,128)(2,1)S(1)} %reshape.4.coup_ref), custom_call_target="tpu_custom_call" | custom-call | flops 30000000 | bytes 12000000 | tf_op jit(solution)/shard_map/pallas_call | solution.py:117
  14.7 0.0 collective-permute-done.lower_ref
  14.7 0.0 collective-permute-done.1.upper_ref
  14.8 0.0 copy-done.1
  14.8 0.0 copy-done.2
  14.8 0.0 copy-done.3
  14.8 2.3 %shard_map.65 = (f32[2,2,12,12,128]{4,3,2,1,0:T(8,128)S(1)}, bf16[2,2,12,12,128]{4,3,2,1,0:T(8,128)(2,1)S(1)}) custom-call(s32[70]{0:T(128)S(1)} %copy-done.1, f32[70]{0:T(128)S(1)} %copy-done.2, f32[70]{0:T(128)S(1)} %copy-done.3, bf16[2,12,16,2304]{3,2,1,0:T(8,128)(2,1)S(1)} %shard_map.64.l_ref, ...), custom_call_target="tpu_custom_call" | custom-call | tf_op jit(solution)/shard_map/pallas_call | solution.py:126
  17.1 4.2 %collective-permute-start.2 = (bf16[2,2,12,12,128]{4,3,2,1,0:T(8,128)(2,1)S(1)}, bf16[2,2,12,12,128]{4,3,2,1,0:T(8,128)(2,1)S(1)}, u32[]{:S(2)}, u32[]{:S(2)}) collective-permute-start(bf16[2,2,12,12,128]{4,3,2,1,0:T(8,128)(2,1)S(1)} %get-tuple-element.8), channel_id=1, source_target_pairs={{0,1},{1,2},{2,3},{4,5},{5,6},{6,7},{8,9},{9,10},{10,11},{12,13},{... | collective-permute-start | bytes 442376 | tf_op jit(solution)/shard_map/ppermute | solution.py:16
  21.3 1.9 %collective-permute-start.3 = (bf16[2,2,12,12,128]{4,3,2,1,0:T(8,128)(2,1)S(1)}, bf16[2,2,12,12,128]{4,3,2,1,0:T(8,128)(2,1)S(1)}, u32[]{:S(2)}, u32[]{:S(2)}) collective-permute-start(bf16[2,2,12,12,128]{4,3,2,1,0:T(8,128)(2,1)S(1)} %get-tuple-element.8), channel_id=1, source_target_pairs={{1,0},{2,1},{3,2},{5,4},{6,5},{7,6},{9,8},{10,9},{11,10},{13,12},{... | collective-permute-start | bytes 442376 | tf_op jit(solution)/shard_map/ppermute | solution.py:16
  23.2 0.7 %collective-permute-done.2 = bf16[2,2,12,12,128]{4,3,2,1,0:T(8,128)(2,1)S(1)} collective-permute-done((bf16[2,2,12,12,128]{4,3,2,1,0:T(8,128)(2,1)S(1)}, bf16[2,2,12,12,128]{4,3,2,1,0:T(8,128)(2,1)S(1)}, u32[]{:S(2)}, u32[]{:S(2)}) %collective-permute-start.2) | collective-permute-done | bytes 147488 | tf_op jit(solution)/shard_map/ppermute | solution.py:16
  23.9 4.4 %collective-permute-done.3 = bf16[2,2,12,12,128]{4,3,2,1,0:T(8,128)(2,1)S(1)} collective-permute-done((bf16[2,2,12,12,128]{4,3,2,1,0:T(8,128)(2,1)S(1)}, bf16[2,2,12,12,128]{4,3,2,1,0:T(8,128)(2,1)S(1)}, u32[]{:S(2)}, u32[]{:S(2)}) %collective-permute-start.3) | collective-permute-done | bytes 147488 | tf_op jit(solution)/shard_map/ppermute | solution.py:16
  28.3 0.1 convert_add_fusion
  28.4 0.9 %copy.17 = f32[2,2,12,12,128]{4,1,3,2,0:T(2,128)} copy(f32[2,2,12,12,128]{4,3,2,1,0:T(8,128)S(1)} %convert_add_fusion) | data formatting | bytes 589824 | tf_op jit(solution)/shard_map/add | solution.py:141
  (1 shorter events, 0.0 us)
Async XLA Ops:
  0.0 9.4 %copy-start = (s32[2,34]{1,0:T(2,128)S(1)}, s32[2,34]{1,0:T(2,128)}, u32[]{:S(2)}) copy-start(s32[2,34]{1,0:T(2,128)} %nb_ref.1) | copy-start | bytes 820
  1.0 13.8 %collective-permute-start = (bf16[2,2,12,12,128]{4,3,2,1,0:T(8,128)(2,1)S(1)}, bf16[2,2,12,12,128]{4,3,2,1,0:T(8,128)(2,1)S(1)}, u32[]{:S(2)}, u32[]{:S(2)}) collective-permute-start(bf16[2,2,12,12,128]{4,3,2,1,0:T(8,128)(2,1)S(1)} %copy.14.own_ref), channel_id=1, source_target_pairs={{0,4},{4,8},{8,12},{12,16},{16,20},{20,24},{24,28},{1,5},{5,9},{9,... | collective-permute-start | bytes 442376 | tf_op jit(solution)/shard_map/ppermute | solution.py:16
  4.1 10.7 %collective-permute-start.1 = (bf16[2,2,12,12,128]{4,3,2,1,0:T(8,128)(2,1)S(1)}, bf16[2,2,12,12,128]{4,3,2,1,0:T(8,128)(2,1)S(1)}, u32[]{:S(2)}, u32[]{:S(2)}) collective-permute-start(bf16[2,2,12,12,128]{4,3,2,1,0:T(8,128)(2,1)S(1)} %copy.14.own_ref), channel_id=1, source_target_pairs={{4,0},{8,4},{12,8},{16,12},{20,16},{24,20},{28,24},{5,1},{9,5},{13... | collective-permute-start | bytes 442376 | tf_op jit(solution)/shard_map/ppermute | solution.py:16
  8.6 6.2 %copy-start.1 = (s32[70]{0:T(128)S(1)}, s32[70]{0:T(128)}, u32[]{:S(2)}) copy-start(s32[70]{0:T(128)} %off_ref.1) | copy-start | bytes 844
  8.6 6.2 %copy-start.2 = (f32[70]{0:T(128)S(1)}, f32[70]{0:T(128)}, u32[]{:S(2)}) copy-start(f32[70]{0:T(128)} %emit_ref.1) | copy-start | bytes 844
  8.6 6.2 %copy-start.3 = (f32[70]{0:T(128)S(1)}, f32[70]{0:T(128)}, u32[]{:S(2)}) copy-start(f32[70]{0:T(128)} %absorb_ref.1) | copy-start | bytes 844
  17.1 6.8 %collective-permute-start.2 = (bf16[2,2,12,12,128]{4,3,2,1,0:T(8,128)(2,1)S(1)}, bf16[2,2,12,12,128]{4,3,2,1,0:T(8,128)(2,1)S(1)}, u32[]{:S(2)}, u32[]{:S(2)}) collective-permute-start(bf16[2,2,12,12,128]{4,3,2,1,0:T(8,128)(2,1)S(1)} %get-tuple-element.8), channel_id=1, source_target_pairs={{0,1},{1,2},{2,3},{4,5},{5,6},{6,7},{8,9},{9,10},{10,11},{12,13},{... | collective-permute-start | bytes 442376 | tf_op jit(solution)/shard_map/ppermute | solution.py:16
  21.3 7.0 %collective-permute-start.3 = (bf16[2,2,12,12,128]{4,3,2,1,0:T(8,128)(2,1)S(1)}, bf16[2,2,12,12,128]{4,3,2,1,0:T(8,128)(2,1)S(1)}, u32[]{:S(2)}, u32[]{:S(2)}) collective-permute-start(bf16[2,2,12,12,128]{4,3,2,1,0:T(8,128)(2,1)S(1)} %get-tuple-element.8), channel_id=1, source_target_pairs={{1,0},{2,1},{3,2},{5,4},{6,5},{7,6},{9,8},{10,9},{11,10},{13,12},{... | collective-permute-start | bytes 442376 | tf_op jit(solution)/shard_map/ppermute | solution.py:16

commit v2 on v1

v2 whole, which is shorter than its diff:
```python
import jax
import jax.numpy as jnp
from jax import lax
from jax.experimental import pallas as pl
from jax.experimental.pallas import tpu as pltpu
from jax.sharding import PartitionSpec as P

F32 = jnp.float32
BF16 = jnp.bfloat16
PAD = 16
CHUNKS = 4


def expanders(orb, width):
    row = lax.broadcasted_iota(jnp.int32, (2 * orb, width), 0)
    col = lax.broadcasted_iota(jnp.int32, (2 * orb, width), 1)
    outer = lax.div(col, 2 * orb)
    inner = lax.div(col - outer * 2 * orb, 2)
    side = col & 1
    part, entry = row & 1, row >> 1
    one, zero = jnp.float32(1), jnp.float32(0)
    at_outer, at_inner = entry == outer, entry == inner
    a1 = jnp.where(at_outer & (part == 0), one, zero)
    a2 = jnp.where(at_outer & (part == 1), one, zero)
    b1 = jnp.where(at_inner & (part == side), one, zero)
    b2 = jnp.where(at_inner & (part != side), jnp.where(side == 0, one, -one), zero)
    return [m.astype(BF16) for m in (a1, a2, b1, b2)]


def split(x):
    high = x.astype(BF16)
    return high, (x - high.astype(F32)).astype(BF16)


def spread_matrix(off_ref, emit_ref, absorb_ref, points):
    span = 2 * points
    lane = lax.broadcasted_iota(jnp.int32, (8, span), 1)

    def add(q, line):
        off = off_ref[q]
        line += jnp.where(lane == span - off, emit_ref[q], jnp.float32(0))
        return line + jnp.where(lane == off, absorb_ref[q], jnp.float32(0))

    line = lax.fori_loop(0, off_ref.shape[0], add, jnp.zeros((8, span), F32))
    full = jnp.broadcast_to(line[0:1], (points, span))
    return pltpu.roll(full, 0, 1, stride=1, stride_axis=0)


def kernel(
    count_a, count_e, orb, listed,
    nb_ref, off_ref, emit_ref, absorb_ref, green_ref, coup_ref,
    out_ref,
    recv_ref, a1_ref, a2_ref, b1_ref, b2_ref, sums_ref, op_ref, toep_ref, side_ref, got_ref,
    near_send, near_recv, far_send, far_recv, side_send, side_recv,
):
    rows, points = green_ref.shape
    width = 2 * orb * orb
    atoms = rows // width
    near = 3 * atoms
    reach = points * 3 // 8
    mine, energy = lax.axis_index("atom"), lax.axis_index("energy")
    odd = lax.rem(mine, 2)
    partner = mine + 1 - 2 * odd
    target = mine + 2 - 4 * odd
    source = mine - 2 + 4 * odd
    has_target = (target >= 0) & (target < count_a)
    has_source = (source >= 0) & (source < count_a)
    has_lower, has_upper = energy > 0, energy < count_e - 1

    barrier = pltpu.get_barrier_semaphore()

    def greet(atom, point):
        pl.semaphore_signal(barrier, inc=1, device_id=(atom, point), device_id_type=pl.DeviceIdType.MESH)

    greet(partner, energy)
    pl.when(has_target)(lambda: greet(target, energy))
    pl.when(has_source)(lambda: greet(source, energy))
    pl.when(has_lower)(lambda: greet(mine, energy - 1))
    pl.when(has_upper)(lambda: greet(mine, energy + 1))
    expected = 1
    for there in (has_target, has_source, has_lower, has_upper):
        expected += there.astype(jnp.int32)
    pl.semaphore_wait(barrier, expected)

    def remote(src, dst, send, recv, atom, point):
        return pltpu.make_async_remote_copy(
            src_ref=src, dst_ref=dst, send_sem=send, recv_sem=recv,
            device_id=(atom, point), device_id_type=pl.DeviceIdType.MESH,
        )

    size = rows // CHUNKS
    near_copies, far_copies = [], []
    for c in range(CHUNKS):
        part = pl.ds(c * size, size)
        near_copies.append(remote(
            green_ref.at[part], recv_ref.at[odd, part], near_send.at[c], near_recv.at[c], partner, energy))
        far_copies.append(remote(
            recv_ref.at[1 - odd, part], recv_ref.at[odd, part], far_send.at[c], far_recv.at[c], target, energy))
    for copy in near_copies:
        copy.start()

    @pl.when(jnp.logical_not(has_source))
    def _():
        recv_ref[odd] = jnp.zeros((rows, points), BF16)

    def forward(chunks):
        for c in chunks:
            near_copies[c].wait_recv()
        for c in chunks:
            pl.when(has_target)(far_copies[c].start)

    mats = expanders(orb, width)
    over_rows = (((0,), (0,)), ((), ()))
    b1_ref[...] = jnp.zeros_like(b1_ref)
    b2_ref[...] = jnp.zeros_like(b2_ref)
    sums_ref[0] = jnp.zeros_like(sums_ref[0])
    first = (mine - 1) * atoms
    for a in range(atoms):
        for i in range(orb):
            start = (a * orb + i) * 2 * orb
            entries = coup_ref[start : start + 2 * orb, :]
            wide = [lax.dot_general(entries, m, over_rows, preferred_element_type=F32) for m in mats]
            a1_ref[i], a2_ref[i] = wide[0], wide[1]
            b1_ref[:, i, :], b2_ref[:, i, :] = wide[2], wide[3]

        def one(k, last):
            b = nb_ref[a, k] - first
            before = jnp.int32(0)
            for x in range(near):
                before = jnp.where(b == x, last[x], before)
            b1, b2 = b1_ref[k], b2_ref[k]
            for i in range(orb):
                sums_ref[k + 1, i] = (
                    sums_ref[before, i] + a1_ref[i, pl.ds(k, 1), :] * b1 + a2_ref[i, pl.ds(k, 1), :] * b2
                )
            return tuple(jnp.where(b == x, k + 1, last[x]) for x in range(near))

        last = (jnp.int32(0),) * near
        last = lax.fori_loop(0, listed // 2, one, last)
        if a == atoms - 1:
            forward(range(CHUNKS // 2, CHUNKS))
        last = lax.fori_loop(listed // 2, listed, one, last)
        for x in range(near):
            op_ref[x, a] = sums_ref[last[x]].astype(BF16)
        if a == 0:
            forward(range(CHUNKS // 2 if atoms > 1 else CHUNKS))
    toep_ref[...] = spread_matrix(off_ref, emit_ref, absorb_ref, points)

    row = lax.broadcasted_iota(jnp.int32, (width, width), 0)
    col = lax.broadcasted_iota(jnp.int32, (width, width), 1)
    even = (row & 1) == 0
    turn = jnp.where(even, (col == row + 1).astype(F32), -(col == row - 1).astype(F32)).astype(BF16)
    height = atoms * orb * PAD

    def apply(block, group):
        total = None
        for a in range(atoms):
            g = block(a)
            turned = jnp.dot(turn, g, preferred_element_type=F32).astype(BF16)
            op = op_ref[group * atoms + a].reshape(height, width)
            term = jnp.dot(op, jnp.concatenate([g, turned], axis=1), preferred_element_type=F32)
            total = term if total is None else total + term
        return total

    p = apply(lambda a: green_ref[a * width : (a + 1) * width], 1)
    p += apply(lambda a: recv_ref[1 - odd, a * width : (a + 1) * width], 2 - 2 * odd)
    for c in range(CHUNKS):
        pl.when(has_source)(far_copies[c].wait_recv)
    p += apply(lambda a: recv_ref[odd, a * width : (a + 1) * width], 2 * odd)

    t_high, t_low = split(toep_ref[...])
    high, low = split(p)

    def spread(r, lanes):
        cut = slice(r * points, (r + 1) * points)
        s = jnp.dot(high[:, cut], t_high[:, lanes], preferred_element_type=F32)
        s += jnp.dot(high[:, cut], t_low[:, lanes], preferred_element_type=F32)
        return s + jnp.dot(low[:, cut], t_high[:, lanes], preferred_element_type=F32)

    ends = slice(points, 2 * points)
    lane = lax.broadcasted_iota(jnp.int32, (height, points), 1)
    end_re = spread(0, ends)
    end_im = pltpu.roll(spread(1, ends), points // 2, 1)
    left = lane < points // 2
    side_ref[0] = jnp.where(left, end_re, end_im).astype(BF16)
    side_ref[1] = jnp.where(left, end_im, end_re).astype(BF16)
    go_up = remote(side_ref.at[0], got_ref.at[0], side_send.at[0], side_recv.at[0], mine, energy + 1)
    go_down = remote(side_ref.at[1], got_ref.at[1], side_send.at[1], side_recv.at[1], mine, energy - 1)
    pl.when(has_upper)(go_up.start)
    pl.when(has_lower)(go_down.start)
    results = [spread(r, slice(0, points)) for r in range(2)]
    pl.when(has_lower)(go_up.wait_recv)
    pl.when(has_upper)(go_down.wait_recv)
    low_end = jnp.where(has_lower, got_ref[0].astype(F32), jnp.float32(0))
    high_end = jnp.where(has_upper, got_ref[1].astype(F32), jnp.float32(0))
    for r in range(2):
        if r:
            low_end = pltpu.roll(low_end, points // 2, 1)
            high_end = pltpu.roll(high_end, points // 2, 1)
        total = results[r] + jnp.where(lane < reach, low_end, jnp.float32(0))
        total += jnp.where(lane >= points - reach, high_end, jnp.float32(0))
        for n in range(atoms * orb):
            out_ref[pl.ds(2 * orb * n + r, orb, stride=2), :] = total[n * PAD : n * PAD + orb]
    for c in range(CHUNKS):
        near_copies[c].wait_send()
        pl.when(has_target)(far_copies[c].wait_send)
    pl.when(has_upper)(go_up.wait_send)
    pl.when(has_lower)(go_down.wait_send)


def shards(green, coupling, neighbours, offsets, w_emit, w_absorb):
    atoms, _, orb, _, points = green.shape
    listed = neighbours.shape[1]
    width = 2 * orb * orb
    rows = atoms * width
    near = 3 * atoms
    height = atoms * orb * PAD
    vmem, smem = pl.BlockSpec(memory_space=pltpu.VMEM), pl.BlockSpec(memory_space=pltpu.SMEM)
    dma = pltpu.SemaphoreType.DMA

    def body(*refs):
        kernel(lax.axis_size("atom"), lax.axis_size("energy"), orb, listed, *refs)

    out = pl.pallas_call(
        body,
        out_shape=jax.ShapeDtypeStruct((rows, points), F32),
        in_specs=[smem] * 4 + [vmem] * 2,
        out_specs=vmem,
        scratch_shapes=[
            pltpu.VMEM((2, rows, points), BF16),
            pltpu.VMEM((orb, listed, width), F32),
            pltpu.VMEM((orb, listed, width), F32),
            pltpu.VMEM((listed, PAD, width), F32),
            pltpu.VMEM((listed, PAD, width), F32),
            pltpu.VMEM((listed + 1, orb, PAD, width), F32),
            pltpu.VMEM((near, atoms, orb, PAD, width), BF16),
            pltpu.VMEM((points, 2 * points), F32),
            pltpu.VMEM((2, height, points), BF16),
            pltpu.VMEM((2, height, points), BF16),
            dma((CHUNKS,)), dma((CHUNKS,)), dma((CHUNKS,)), dma((CHUNKS,)), dma((2,)), dma((2,)),
        ],
        compiler_params=pltpu.CompilerParams(
            collective_id=0, has_side_effects=True, vmem_limit_bytes=40 << 20
        ),
    )(
        neighbours, offsets, w_emit, w_absorb,
        green.transpose(0, 2, 3, 1, 4).reshape(rows, points),
        coupling.transpose(0, 3, 4, 2, 1).reshape(rows, listed),
    )
    return out.reshape(atoms, orb, orb, 2, points).transpose(0, 3, 1, 2, 4)


def solution(mesh):
    return jax.shard_map(
        shards,
        mesh=mesh,
        in_specs=(
            P("atom", None, None, None, "energy"),
            P("atom", None, None, None, None),
            P("atom", None),
            P(),
            P(),
            P(),
        ),
        out_specs=P("atom", None, None, None, "energy"),
        check_vma=False,
    )
```

time: 29.6 us -> 22 us (0.74)
  the two profiles are of different devices: /device:TPU:9 before, /device:TPU:1 now
where the time goes in v2:
time: 22 us; the launch traced here: 21.8 us
  Pallas kernels  18.6 us (85%)
  local copies, waits for them, and re-layouts  3.24 us (15%)
    pallas_call x1, Pallas kernels, shards(): pl.pallas_call(body, out_shape=jax.ShapeDtypeStruct((rows, points), F32),...  18.6 us
    unnamed x13, local copies, waits for them, and re-layouts  3.24 us

profile of v2, /device:TPU:1, one launch (start us, length us, event | category | flops | bytes accessed | tf_op | source)
XLA Modules:
  0.0 21.8 jit_solution(18170274235762406114)
XLA Ops:
  0.0 0.0 copy-start.4
  0.0 0.0 copy-start.5
  0.0 0.0 copy-start.2
  0.0 0.0 copy-start.3
  0.0 0.6 %copy-done.4 = f32[70]{0:T(128)S(1)} copy-done((f32[70]{0:T(128)S(1)}, f32[70]{0:T(128)}, u32[]{:S(2)}) %copy-start.4) | copy-done | bytes 304
  0.7 0.0 copy-done.5
  0.7 0.0 copy-done.2
  0.7 0.0 copy-done.3
  0.7 0.0 copy-start
  0.7 0.9 %copy-done = bf16[2,2,12,12,128]{4,1,3,2,0:T(2,128)(2,1)S(1)} copy-done((bf16[2,2,12,12,128]{4,1,3,2,0:T(2,128)(2,1)S(1)}, bf16[2,2,12,12,128]{4,1,3,2,0:T(2,128)(2,1)}, u32[]{:S(2)}) %copy-start) | copy-done | bytes 147480
  1.6 0.0 copy-start.1
  1.6 0.9 %copy-done.1 = bf16[2,34,2,12,12]{1,2,4,3,0:T(2,128)(2,1)S(1)} copy-done((bf16[2,34,2,12,12]{1,2,4,3,0:T(2,128)(2,1)S(1)}, bf16[2,34,2,12,12]{1,2,4,3,0:T(2,128)(2,1)}, u32[]{:S(2)}) %copy-start.1) | copy-done | bytes 39192
  2.5 18.6 %shard_map.64 = f32[576,128]{1,0:T(8,128)S(1)} custom-call(s32[2,34]{1,0:T(2,128)S(1)} %copy-done.2, s32[70]{0:T(128)S(1)} %copy-done.3, f32[70]{0:T(128)S(1)} %copy-done.4, f32[70]{0:T(128)S(1)} %copy-done.5, bf16[576,128]{1,0:T(8,128)(2,1)S(1)} %bitcast.10, bf16[576,34]{1,0:T(8,128)(2,1)S(1)} %bitcast.11), custom_call_target="tpu_custom_call" | custom-call | tf_op jit(solution)/shard_map/pallas_call | solution.py:224
  21.1 0.7 %copy.8 = f32[2,2,12,12,128]{4,1,3,2,0:T(2,128)} copy(f32[2,2,12,12,128]{4,1,3,2,0:T(2,128)S(1)} %bitcast.9) | data formatting | bytes 589824
Async XLA Ops:
  0.0 0.7 %copy-start.4 = (f32[70]{0:T(128)S(1)}, f32[70]{0:T(128)}, u32[]{:S(2)}) copy-start(f32[70]{0:T(128)} %refs_2_.1) | copy-start | bytes 844
  0.0 0.7 %copy-start.5 = (f32[70]{0:T(128)S(1)}, f32[70]{0:T(128)}, u32[]{:S(2)}) copy-start(f32[70]{0:T(128)} %refs_3_.1) | copy-start | bytes 844
  0.0 0.7 %copy-start.2 = (s32[2,34]{1,0:T(2,128)S(1)}, s32[2,34]{1,0:T(2,128)}, u32[]{:S(2)}) copy-start(s32[2,34]{1,0:T(2,128)} %refs_0_.1) | copy-start | bytes 820
  0.0 0.7 %copy-start.3 = (s32[70]{0:T(128)S(1)}, s32[70]{0:T(128)}, u32[]{:S(2)}) copy-start(s32[70]{0:T(128)} %refs_1_.1) | copy-start | bytes 844
  0.7 0.9 %copy-start = (bf16[2,2,12,12,128]{4,1,3,2,0:T(2,128)(2,1)S(1)}, bf16[2,2,12,12,128]{4,1,3,2,0:T(2,128)(2,1)}, u32[]{:S(2)}) copy-start(bf16[2,2,12,12,128]{4,1,3,2,0:T(2,128)(2,1)} %param.6) | copy-start | bytes 442372
  1.6 0.9 %copy-start.1 = (bf16[2,34,2,12,12]{1,2,4,3,0:T(2,128)(2,1)S(1)}, bf16[2,34,2,12,12]{1,2,4,3,0:T(2,128)(2,1)}, u32[]{:S(2)}) copy-start(bf16[2,34,2,12,12]{1,2,4,3,0:T(2,128)(2,1)} %param.7) | copy-start | bytes 117508

commit v3 on v2

--- a/solution.py
+++ b/solution.py
@@ -9,6 +9,7 @@
 BF16 = jnp.bfloat16
 PAD = 16
 CHUNKS = 4
+GROUP = 4
 
 
 def expanders(orb, width):
@@ -41,7 +42,7 @@
         line += jnp.where(lane == span - off, emit_ref[q], jnp.float32(0))
         return line + jnp.where(lane == off, absorb_ref[q], jnp.float32(0))
 
-    line = lax.fori_loop(0, off_ref.shape[0], add, jnp.zeros((8, span), F32))
+    line = lax.fori_loop(0, off_ref.shape[0], add, jnp.zeros((8, span), F32), unroll=True)
     full = jnp.broadcast_to(line[0:1], (points, span))
     return pltpu.roll(full, 0, 1, stride=1, stride_axis=0)
 
@@ -50,7 +51,7 @@
     count_a, count_e, orb, listed,
     nb_ref, off_ref, emit_ref, absorb_ref, green_ref, coup_ref,
     out_ref,
-    recv_ref, a1_ref, a2_ref, b1_ref, b2_ref, sums_ref, op_ref, toep_ref, side_ref, got_ref,
+    recv_ref, a1_ref, a2_ref, b1_ref, b2_ref, flat_ref, sums_ref, op_ref, toep_ref, side_ref, got_ref,
     near_send, near_recv, far_send, far_recv, side_send, side_recv,
 ):
     rows, points = green_ref.shape
@@ -110,18 +111,24 @@
             pl.when(has_target)(far_copies[c].start)
 
     mats = expanders(orb, width)
+    same = lax.broadcasted_iota(jnp.int32, (2 * orb, 2 * orb), 0) == lax.broadcasted_iota(
+        jnp.int32, (2 * orb, 2 * orb), 1
+    )
+    same = same.astype(F32).astype(BF16)
     over_rows = (((0,), (0,)), ((), ()))
-    b1_ref[...] = jnp.zeros_like(b1_ref)
-    b2_ref[...] = jnp.zeros_like(b2_ref)
+    flat_ref[...] = jnp.zeros_like(flat_ref)
     sums_ref[0] = jnp.zeros_like(sums_ref[0])
     first = (mine - 1) * atoms
     for a in range(atoms):
         for i in range(orb):
             start = (a * orb + i) * 2 * orb
             entries = coup_ref[start : start + 2 * orb, :]
-            wide = [lax.dot_general(entries, m, over_rows, preferred_element_type=F32) for m in mats]
-            a1_ref[i], a2_ref[i] = wide[0], wide[1]
-            b1_ref[:, i, :], b2_ref[:, i, :] = wide[2], wide[3]
+            flat_ref[pl.ds(i, listed, stride=PAD), :] = lax.dot_general(
+                entries, same, over_rows, preferred_element_type=F32
+            )
+        flat = flat_ref[...].astype(BF16)
+        for mat, ref in zip(mats, (a1_ref, a2_ref, b1_ref, b2_ref)):
+            ref[...] = jnp.dot(flat, mat, preferred_element_type=F32).reshape(ref.shape)
 
         def one(k, last):
             b = nb_ref[a, k] - first
@@ -129,10 +136,14 @@
             for x in range(near):
                 before = jnp.where(b == x, last[x], before)
             b1, b2 = b1_ref[k], b2_ref[k]
-            for i in range(orb):
-                sums_ref[k + 1, i] = (
-                    sums_ref[before, i] + a1_ref[i, pl.ds(k, 1), :] * b1 + a2_ref[i, pl.ds(k, 1), :] * b2
-                )
+            for start in range(0, orb, GROUP):
+                group = range(start, min(start + GROUP, orb))
+                old = [sums_ref[before, i] for i in group]
+                new = [
+                    o + a1_ref[k, i : i + 1, :] * b1 + a2_ref[k, i : i + 1, :] * b2 for o, i in zip(old, group)
+                ]
+                for i, value in zip(group, new):
+                    sums_ref[k + 1, i] = value
             return tuple(jnp.where(b == x, k + 1, last[x]) for x in range(near))
 
         last = (jnp.int32(0),) * near
@@ -228,10 +239,11 @@
         out_specs=vmem,
         scratch_shapes=[
             pltpu.VMEM((2, rows, points), BF16),
-            pltpu.VMEM((orb, listed, width), F32),
-            pltpu.VMEM((orb, listed, width), F32),
-            pltpu.VMEM((listed, PAD, width), F32),
-            pltpu.VMEM((listed, PAD, width), F32),
+            pltpu.VMEM((listed, PAD, width), F32),
+            pltpu.VMEM((listed, PAD, width), F32),
+            pltpu.VMEM((listed, PAD, width), F32),
+            pltpu.VMEM((listed, PAD, width), F32),
+            pltpu.VMEM((listed * PAD, 2 * orb), F32),
             pltpu.VMEM((listed + 1, orb, PAD, width), F32),
             pltpu.VMEM((near, atoms, orb, PAD, width), BF16),
             pltpu.VMEM((points, 2 * points), F32),

time: 22 us -> 20.4 us (0.927)
  the two profiles are of different devices: /device:TPU:1 before, /device:TPU:9 now
where the time goes in v3:
time: 20.4 us; the launch traced here: 20.1 us
  Pallas kernels  16.9 us (83%)
  local copies, waits for them, and re-layouts  3.24 us (16%)
    pallas_call x1, Pallas kernels, shards(): pl.pallas_call(body, out_shape=jax.ShapeDtypeStruct((rows, points), F32),...  16.9 us
    unnamed x13, local copies, waits for them, and re-layouts  3.24 us

profile of v3, /device:TPU:9, one launch (start us, length us, event | category | flops | bytes accessed | tf_op | source)
XLA Modules:
  0.0 20.1 jit_solution(4644670409740092783)
XLA Ops:
  0.0 0.0 copy-start.4
  0.0 0.0 copy-start.5
  0.0 0.0 copy-start.2
  0.0 0.0 copy-start.3
  0.0 0.6 %copy-done.4 = f32[70]{0:T(128)S(1)} copy-done((f32[70]{0:T(128)S(1)}, f32[70]{0:T(128)}, u32[]{:S(2)}) %copy-start.4) | copy-done | bytes 304
  0.7 0.0 copy-done.5
  0.7 0.0 copy-done.2
  0.7 0.0 copy-done.3
  0.7 0.0 copy-start
  0.7 0.9 %copy-done = bf16[2,2,12,12,128]{4,1,3,2,0:T(2,128)(2,1)S(1)} copy-done((bf16[2,2,12,12,128]{4,1,3,2,0:T(2,128)(2,1)S(1)}, bf16[2,2,12,12,128]{4,1,3,2,0:T(2,128)(2,1)}, u32[]{:S(2)}) %copy-start) | copy-done | bytes 147480
  1.6 0.0 copy-start.1
  1.6 0.9 %copy-done.1 = bf16[2,34,2,12,12]{1,2,4,3,0:T(2,128)(2,1)S(1)} copy-done((bf16[2,34,2,12,12]{1,2,4,3,0:T(2,128)(2,1)S(1)}, bf16[2,34,2,12,12]{1,2,4,3,0:T(2,128)(2,1)}, u32[]{:S(2)}) %copy-start.1) | copy-done | bytes 39192
  2.5 16.9 %shard_map.64 = f32[576,128]{1,0:T(8,128)S(1)} custom-call(s32[2,34]{1,0:T(2,128)S(1)} %copy-done.2, s32[70]{0:T(128)S(1)} %copy-done.3, f32[70]{0:T(128)S(1)} %copy-done.4, f32[70]{0:T(128)S(1)} %copy-done.5, bf16[576,128]{1,0:T(8,128)(2,1)S(1)} %bitcast.10, bf16[576,34]{1,0:T(8,128)(2,1)S(1)} %bitcast.11), custom_call_target="tpu_custom_call" | custom-call | tf_op jit(solution)/shard_map/pallas_call | solution.py:235
  19.4 0.7 %copy.8 = f32[2,2,12,12,128]{4,1,3,2,0:T(2,128)} copy(f32[2,2,12,12,128]{4,1,3,2,0:T(2,128)S(1)} %bitcast.9) | data formatting | bytes 589824
Async XLA Ops:
  0.0 0.7 %copy-start.4 = (f32[70]{0:T(128)S(1)}, f32[70]{0:T(128)}, u32[]{:S(2)}) copy-start(f32[70]{0:T(128)} %refs_2_.1) | copy-start | bytes 844
  0.0 0.7 %copy-start.5 = (f32[70]{0:T(128)S(1)}, f32[70]{0:T(128)}, u32[]{:S(2)}) copy-start(f32[70]{0:T(128)} %refs_3_.1) | copy-start | bytes 844
  0.0 0.7 %copy-start.2 = (s32[2,34]{1,0:T(2,128)S(1)}, s32[2,34]{1,0:T(2,128)}, u32[]{:S(2)}) copy-start(s32[2,34]{1,0:T(2,128)} %refs_0_.1) | copy-start | bytes 820
  0.0 0.7 %copy-start.3 = (s32[70]{0:T(128)S(1)}, s32[70]{0:T(128)}, u32[]{:S(2)}) copy-start(s32[70]{0:T(128)} %refs_1_.1) | copy-start | bytes 844
  0.7 0.9 %copy-start = (bf16[2,2,12,12,128]{4,1,3,2,0:T(2,128)(2,1)S(1)}, bf16[2,2,12,12,128]{4,1,3,2,0:T(2,128)(2,1)}, u32[]{:S(2)}) copy-start(bf16[2,2,12,12,128]{4,1,3,2,0:T(2,128)(2,1)} %param.6) | copy-start | bytes 442372
  1.6 0.9 %copy-start.1 = (bf16[2,34,2,12,12]{1,2,4,3,0:T(2,128)(2,1)S(1)}, bf16[2,34,2,12,12]{1,2,4,3,0:T(2,128)(2,1)}, u32[]{:S(2)}) copy-start(bf16[2,34,2,12,12]{1,2,4,3,0:T(2,128)(2,1)} %param.7) | copy-start | bytes 117508
